TPU v7x, 32 devices: a whole 2x2x4 slice. The times are simulated.
32 devices in a mesh: row: 16 (over z, x, core), col: 2 (over y).
Axes of the slice: x: 2, y: 2, z: 4, core: 2. Of those that a mesh axis runs over, the one named last changes fastest.
Arguments:
- vectors: bfloat16 [8, 32768], P(None, ('row', 'col')), may hold values from -6 to 6
- energies: float32 [32768], P(('row', 'col')), may hold values from 0.5 to 6
- tiles: bfloat16 [32768, 4096], P(('row', 'col')), may hold values from -0.25 to 0.25
- tile_rows: int32 [32768], P(('row', 'col')), may hold values from 0 to 31, as said below
- tile_cols: int32 [32768], P(('row', 'col')), may hold values from 0 to 255
- tile_count: int32 [32], P(('row', 'col')), may hold values from 128 to 1024, as said below
Outputs:
- product: bfloat16 [8, 32768], P(None, ('row', 'col'))
- residual: float32 [8, 32768], P(None, ('row', 'col'))
Inputs may be any that keep to these rules, and one draw needn't show every extreme that they name: `tile_count`: every count is at least 128, and some device uses all 1024 slots in every draw; a few devices are full while most use far fewer. `tile_rows`: slots may name the same row and column block more than once; such tiles add.
All inputs are finite; a program needn't handle non-finite values.
Results may differ from a plain program's by a relative error of at most 0.008.
Values may be sent and summed in bfloat16 or wider, within the bound.
No kernel may reach another device: no remote copies, remote signals or barrier semaphores. Data moves between devices by JAX's collectives and lax.ppermute only.
A program may use at most 64 MiB of HBM per device.

v0:
```python
import functools
import math

import jax
import jax.numpy as jnp
from jax import lax
from jax.experimental import pallas as pl
from jax.experimental.pallas import tpu as pltpu
from jax.sharding import Mesh, PartitionSpec as P

LANES = 128
SUB = 8
CHUNK = 64

NT = (((1,), (1,)), ((), ()))


def tile_kernel(
    n_core, n_col, side, count_s, rows_h, cols_h, ener_h, tiles, *refs,
):
    gath, refs = refs[:n_core], refs[n_core:]
    (own_ref, send_ref, rest_ref, rows_s, cols_s, ener,
     buf, table, picked, select, part, sems, small, *acc) = refs
    n_far, kvec, own = gath[0].shape
    slots = tiles.shape[0]
    blk_own = own // side
    per = LANES // side
    n_chunk = tiles.shape[1] // LANES
    my_far, my_core, my_col = (lax.axis_index(name) for name in ("far", "core", "col"))

    copies = [
        pltpu.make_async_copy(src, dst, small.at[i])
        for i, (src, dst) in enumerate(
            ((cols_h, cols_s), (rows_h, rows_s), (ener_h, ener))
        )
    ]
    for copy in copies:
        copy.start()

    def tile_copy(ch):
        span = pl.ds(pl.multiple_of(ch * CHUNK, CHUNK), CHUNK)
        return pltpu.make_async_copy(tiles.at[span], buf.at[span], sems.at[ch])

    count = count_s[0]
    used = (count + CHUNK - 1) // CHUNK

    def start(ch, carry):
        tile_copy(ch).start()
        return carry

    lax.fori_loop(0, used, start, 0)

    lane = lax.broadcasted_iota(jnp.int32, (kvec, LANES), 1)
    low = lane < side
    zero = jnp.zeros((kvec, LANES), jnp.float32)

    for s in range(n_core):
        core = lax.rem(my_core + (n_core - s), n_core)
        for f in range(n_far):
            for p in range(own // LANES):
                x = gath[s][f, :, p * LANES:(p + 1) * LANES].astype(jnp.float32)
                y = pltpu.roll(x, side, 1)
                at = (f * n_core + core) * blk_own + p * per
                even = jnp.concatenate([jnp.where(low, x, zero), jnp.where(low, zero, y)], axis=0)
                odd = jnp.concatenate([jnp.where(low, y, zero), jnp.where(low, zero, x)], axis=0)
                table[at] = even.astype(jnp.bfloat16)
                table[at + 1] = odd.astype(jnp.bfloat16)
    n_blocks = n_far * n_core * blk_own
    table[n_blocks] = jnp.zeros((per * kvec, LANES), jnp.bfloat16)

    for copy in copies:
        copy.wait()
    n_seg = acc[0].shape[0]
    width = n_chunk * SUB

    def clear(r, carry):
        for a in acc:
            a[r] = jnp.zeros(a.shape[1:], jnp.float32)
        return carry

    lax.fori_loop(0, n_seg, clear, 0)

    k_id = lax.broadcasted_iota(jnp.int32, (width, LANES), 0)
    n_id = lax.broadcasted_iota(jnp.int32, (width, LANES), 1)
    base_id = n_id - per * (k_id // SUB)
    for par in range(per):
        for jp in range(per):
            at = (par * per + jp) * width
            hit = (base_id == side * par + jp).astype(jnp.float32)
            select[at:at + width, :] = hit.astype(jnp.bfloat16)

    rows_of = per * kvec

    def product(base, half, x):
        xh = x[half * SUB:(half + 1) * SUB]
        w = jnp.concatenate(
            [xh[:, c * LANES:(c + 1) * LANES] for c in range(n_chunk)], axis=0
        ).astype(jnp.bfloat16)
        entries = []
        for t in range(SUB):
            slot = base + half * SUB + t
            entries.append(table[jnp.where(slot < count, cols_s[slot], n_blocks)])
        left = jnp.concatenate(entries, axis=0)
        return lax.dot_general(left, w, NT, preferred_element_type=jnp.float32)

    def accumulate(at, out):
        for t in range(SUB):
            r = rows_s[at + t]
            acc[t][r] += out[t * rows_of:(t + 1) * rows_of]

    def one_chunk(ch, carry):
        tile_copy(ch).wait()
        waiting = None
        for q in range(CHUNK // (2 * SUB)):
            base = pl.multiple_of(ch * CHUNK + q * 2 * SUB, 2 * SUB)
            x = buf[pl.ds(base, 2 * SUB), :].astype(jnp.float32)
            for half in range(2):
                out = product(base, half, x)
                if waiting is not None:
                    accumulate(*waiting)
                waiting = (base + half * SUB, out)
        accumulate(*waiting)
        return carry

    lax.fori_loop(0, used, one_chunk, 0)

    lane_w = lax.broadcasted_iota(jnp.int32, (rows_of, width), 1) % SUB
    pairs = n_seg // per

    def pick(m, carry):
        pieces = []
        for par in range(per):
            total = jnp.zeros((rows_of, width), jnp.float32)
            for t in range(SUB):
                total = jnp.where(lane_w == t, acc[t][m * per + par], total)
            for jp in range(per):
                pieces.append(total[jp * kvec:(jp + 1) * kvec])
        a = jnp.concatenate(pieces, axis=1)
        hi = a.astype(jnp.bfloat16).astype(jnp.float32)
        both = jnp.concatenate([hi, a - hi], axis=0).astype(jnp.bfloat16)
        picked[pl.ds(pl.multiple_of(m * 2 * kvec, 2 * kvec), 2 * kvec), :] = both
        return carry

    lax.fori_loop(0, pairs, pick, 0)

    spread = jnp.dot(picked[...], select[...], preferred_element_type=jnp.float32)
    for m in range(pairs):
        at = m * 2 * kvec
        row = spread[at:at + kvec] + spread[at + kvec:at + 2 * kvec]
        c, lane0 = divmod(m * LANES, own)
        part[c, :, lane0:lane0 + LANES] = row

    own_ref[...] = part[my_col] + ener[...] * gath[0][my_far].astype(jnp.float32)
    for s in range(1, n_col):
        share = part[lax.rem(my_col + s, n_col)]
        send_ref[s - 1] = share.astype(jnp.bfloat16)
        rest_ref[s - 1] = share


def tile_work(rows, cols, count, gath, n_col, ener, tiles):
    n_core = len(gath)
    n_far, kvec, own = gath[0].shape
    slots, area = tiles.shape
    side = math.isqrt(area)
    per = LANES // side
    blk_own = own // side
    n_seg = n_col * blk_own
    width = area // LANES * SUB
    vmem = pl.BlockSpec(memory_space=pltpu.VMEM)
    far_away = pl.BlockSpec(memory_space=pltpu.HBM)
    return pl.pallas_call(
        functools.partial(tile_kernel, n_core, n_col, side),
        out_shape=(
            jax.ShapeDtypeStruct((kvec, own), jnp.float32),
            jax.ShapeDtypeStruct((n_col - 1, kvec, own), jnp.bfloat16),
            jax.ShapeDtypeStruct((n_col - 1, kvec, own), jnp.float32),
        ),
        in_specs=[pl.BlockSpec(memory_space=pltpu.SMEM)] + [far_away] * 4 + [vmem] * n_core,
        out_specs=(vmem, vmem, vmem),
        scratch_shapes=[
            pltpu.SMEM((slots,), jnp.int32),
            pltpu.SMEM((slots,), jnp.int32),
            pltpu.VMEM((1, own), jnp.float32),
            pltpu.VMEM((slots, area), jnp.bfloat16),
            pltpu.VMEM((n_far * n_core * blk_own + 1, per * kvec, LANES), jnp.bfloat16),
            pltpu.VMEM((n_seg // per * 2 * kvec, per * per * width), jnp.bfloat16),
            pltpu.VMEM((per * per * width, LANES), jnp.bfloat16),
            pltpu.VMEM((n_col, kvec, own), jnp.float32),
            pltpu.SemaphoreType.DMA((slots // CHUNK,)),
            pltpu.SemaphoreType.DMA((3,)),
        ] + [pltpu.VMEM((n_seg, per * kvec, width), jnp.float32)] * SUB,
        compiler_params=pltpu.CompilerParams(vmem_limit_bytes=48 * 2**20),
        cost_estimate=pl.CostEstimate(
            flops=2 * slots * area * kvec, bytes_accessed=2 * slots * area, transcendentals=0
        ),
        name="tile_work",
    )(count, *[pltpu.with_memory_space_constraint(x, pltpu.HBM) for x in (rows, cols, ener, tiles)],
      *gath)


def terms_kernel(own, rest, vec, *refs):
    others, (terms_ref, wide) = refs[:-2], refs[-2:]
    n_col = len(others) + 1
    kvec = vec.shape[0]

    def outer(share, seg):
        return lax.dot_general(
            share, seg[...].astype(jnp.float32), NT,
            precision=lax.Precision.HIGHEST, preferred_element_type=jnp.float32,
        )

    terms = outer(own[...], vec)
    for s in range(1, n_col):
        terms = terms + outer(rest[s - 1], others[n_col - s - 1])
    wide[...] = jnp.zeros(wide.shape, jnp.float32)
    wide[:, :kvec] = terms
    spaced = pltpu.roll(wide[...], 0, 1, stride=kvec, stride_axis=0)
    flat = jnp.sum(spaced, axis=0, keepdims=True)
    for i in range(terms_ref.shape[0]):
        terms_ref[i] = flat


def gram_terms(own, rest, vectors, others, members):
    vmem = pl.BlockSpec(memory_space=pltpu.VMEM)
    return pl.pallas_call(
        terms_kernel,
        out_shape=jax.ShapeDtypeStruct((members, 1, LANES), jnp.float32),
        in_specs=[vmem] * (3 + len(others)),
        out_specs=vmem,
        scratch_shapes=[pltpu.VMEM((vectors.shape[0], LANES), jnp.float32)],
        compiler_params=pltpu.CompilerParams(vmem_limit_bytes=4 * 2**20),
        name="gram_terms",
    )(own, rest, vectors, *others)


def finish_kernel(scale, base, gram_parts, vec, *refs):
    got, (product, residual) = refs[:-2], refs[-2:]
    whole = base[...]
    for piece in got:
        whole = whole + piece[...].astype(jnp.float32)
    product[...] = whole.astype(jnp.bfloat16)
    flat = gram_parts[0]
    for i in range(1, gram_parts.shape[0]):
        flat = flat + gram_parts[i]
    kvec = vec.shape[0]
    lane = lax.broadcasted_iota(jnp.int32, (kvec, LANES), 1)
    first = kvec * lax.broadcasted_iota(jnp.int32, (kvec, LANES), 0)
    wide = jnp.broadcast_to(flat * scale, (kvec, LANES))
    vec32 = vec[...].astype(jnp.float32)
    for a in range(kvec):
        column = jnp.sum(jnp.where(lane == first + a, wide, 0.0), axis=1, keepdims=True)
        whole = whole - column * vec32[a:a + 1, :]
    residual[...] = whole


def finish(scale, base, gram_parts, vectors, got):
    vmem = pl.BlockSpec(memory_space=pltpu.VMEM)
    return pl.pallas_call(
        functools.partial(finish_kernel, scale),
        out_shape=(
            jax.ShapeDtypeStruct(vectors.shape, jnp.bfloat16),
            jax.ShapeDtypeStruct(vectors.shape, jnp.float32),
        ),
        in_specs=[vmem] * (3 + len(got)),
        out_specs=(vmem, vmem),
        compiler_params=pltpu.CompilerParams(vmem_limit_bytes=4 * 2**20),
        name="finish",
    )(base, gram_parts, vectors, *got)


def from_all(x, axis):
    size = lax.axis_size(axis)
    got = [x]
    for s in range(1, size):
        got.append(lax.ppermute(x, axis, [(i, (i + s) % size) for i in range(size)]))
    return got


def copies_kernel(x, out, sems):
    copies = [pltpu.make_async_copy(x, out.at[i], sems.at[i]) for i in range(out.shape[0])]
    for copy in copies:
        copy.start()
    for copy in copies:
        copy.wait()


def repeat(x, size):
    return pl.pallas_call(
        copies_kernel,
        out_shape=jax.ShapeDtypeStruct((size,) + x.shape, x.dtype),
        in_specs=[pl.BlockSpec(memory_space=pltpu.HBM)],
        out_specs=pl.BlockSpec(memory_space=pltpu.VMEM),
        scratch_shapes=[pltpu.SemaphoreType.DMA((size,))],
        compiler_params=pltpu.CompilerParams(vmem_limit_bytes=4 * 2**20),
        name="copies",
    )(pltpu.with_memory_space_constraint(x, pltpu.HBM))


def per_device(vectors, energies, tiles, tile_rows, tile_cols, tile_count):
    kvec, own = vectors.shape
    n_col = lax.axis_size("col")
    gath = lax.all_to_all(repeat(vectors, lax.axis_size("far")), "far", 0, 0)
    gath = from_all(gath, "core")
    base, send, rest = tile_work(
        tile_rows, tile_cols, tile_count, gath, n_col, energies[None, :], tiles
    )
    got = [
        lax.ppermute(send[s - 1], "col", [(c, (c + s) % n_col) for c in range(n_col)])
        for s in range(1, n_col)
    ]
    others = from_all(vectors, "col")[1:]
    members = lax.axis_size(("far", "core", "col"))
    terms = gram_terms(base, rest, vectors, others, members)
    gram_parts = lax.all_to_all(terms, ("far", "core", "col"), 0, 0)
    return finish(1.0 / (members * own), base, gram_parts, vectors, got)


def solution(mesh):
    n_row, n_col = mesh.devices.shape
    n_core = 2 if n_row % 2 == 0 else 1
    split = ("far", "core", "col")
    chips = Mesh(mesh.devices.reshape(n_row // n_core, n_core, n_col), split)
    in_specs = (P(None, split), P(split), P(split, None), P(split), P(split), P(split))
    out_specs = (P(None, split), P(None, split))
    return jax.shard_map(
        per_device, mesh=chips, in_specs=in_specs, out_specs=out_specs, check_vma=False
    )
```

profile of v0, /device:TPU:0, one launch (start us, length us, event | category | flops | bytes accessed | tf_op | source)
XLA Modules:
  0.0 35.6 jit_solution(10799881824718577448)
XLA Ops:
  0.6 0.0 copy-start
  0.6 1.1 %copies.1 = bf16[8,8,1024]{2,1,0:T(8,128)(2,1)S(1)} custom-call(bf16[8,1024]{1,0:T(8,128)(2,1)} %vec.3), custom_call_target="tpu_custom_call" | custom-call | tf_op jit(solution)/shard_map/copies/pallas_call | solution.py:288
  1.8 14.4 %all_to_all.10.refs_0_ = bf16[8,8,1024]{2,1,0:T(8,128)(2,1)S(1)} all-to-all(bf16[8,8,1024]{2,1,0:T(8,128)(2,1)S(1)} %copies.1), channel_id=1, replica_groups=mesh['far'=8,'core'=2,'col'=2] {'far'}, dimensions={0} | all-to-all | bytes 262144 | tf_op jit(solution)/shard_map/all_to_all | solution.py:302
  16.1 0.0 collective-permute-start
  16.1 1.5 %collective-permute-start.1 = (bf16[8,1024]{1,0:T(8,128)(2,1)}, bf16[8,1024]{1,0:T(8,128)(2,1)S(1)}, u32[]{:S(2)}, u32[]{:S(2)}) collective-permute-start(bf16[8,1024]{1,0:T(8,128)(2,1)} %vec.3), channel_id=1, source_target_pairs={{0,1},{1,0},{2,3},{3,2},{4,5},{5,4},{6,7},{7,6},{8,9},{9,8},{10,11... | collective-permute-start | bytes 49160 | tf_op jit(solution)/shard_map/ppermute | solution.py:275
  18.3 0.0 collective-permute-done.refs_1_
  18.3 3.2 %tile_work.1 = (f32[8,1024]{1,0:T(8,128)S(1)}, bf16[1,8,1024]{2,1,0:T(8,128)(2,1)S(1)}, f32[1,8,1024]{2,1,0:T(8,128)S(1)}) custom-call(s32[1]{0:T(128)S(6)} %copy.8.count_s, s32[1024]{0:T(1024)} %rows_h.1, s32[1024]{0:T(1024)} %cols_h.1, f32[1,1024]{1,0:T(1,128)} %bitcast.3, bf16[1024,4096]{1,0:T(8,128)(2,1)} %tiles.1, ...), custom_call_target="tpu_custom_call" | custom-call | flops 67108864 | bytes 8388608 | tf_op jit(solution)/shard_map/tile_work/pallas_call | solution.py:171
  21.6 0.0 collective-permute-done.1.refs_0_
  21.6 0.0 copy-done
  21.6 0.9 %gram_terms.1 = f32[32,1,128]{2,1,0:T(1,128)} custom-call(f32[8,1024]{1,0:T(8,128)S(1)} %get-tuple-element.5.own.base, f32[1,8,1024]{2,1,0:T(8,128)S(1)} %get-tuple-element.6.rest, bf16[8,1024]{1,0:T(8,128)(2,1)S(1)} %copy-done, bf16[8,1024]{1,0:T(8,128)(2,1)S(1)} %collective-permute-done.1.refs_0_), custom_call_target="tpu_custom_call" | custom-call | tf_op jit(solution)/shard_map/gram_terms/pallas_call | solution.py:225
  22.5 5.2 %all-to-all-start.1 = ((f32[32,1,128]{2,1,0:T(1,128)}), f32[32,1,128]{2,1,0:T(1,128)S(1)}, u32[]{:S(2)}, u32[]{:S(2)}) async-start(f32[32,1,128]{2,1,0:T(1,128)} %gram_terms.1), calls=%async_computation.1 | async-start | bytes 32768 | tf_op jit(solution)/shard_map/all_to_all | solution.py:314
  27.7 1.8 %collective-permute-start.2 = (bf16[8,1024]{1,0:T(8,128)(2,1)S(1)}, bf16[8,1024]{1,0:T(8,128)(2,1)S(1)}, u32[]{:S(2)}, u32[]{:S(2)}) collective-permute-start(bf16[8,1024]{1,0:T(8,128)(2,1)S(1)} %bitcast.2), channel_id=1, source_target_pairs={{0,1},{1,0},{2,3},{3,2},{4,5},{5,4},{6,7},{7,6},{8,9},{9,8},{10,11... | collective-permute-start | bytes 49160 | tf_op jit(solution)/shard_map/ppermute | solution.py:308
  29.6 2.0 %collective-permute-done.2.refs_0_ = bf16[8,1024]{1,0:T(8,128)(2,1)S(1)} collective-permute-done((bf16[8,1024]{1,0:T(8,128)(2,1)S(1)}, bf16[8,1024]{1,0:T(8,128)(2,1)S(1)}, u32[]{:S(2)}, u32[]{:S(2)}) %collective-permute-start.2) | collective-permute-done | bytes 16416 | tf_op jit(solution)/shard_map/ppermute | solution.py:308
  31.6 3.3 %all-to-all-done.1.gram_parts = f32[32,1,128]{2,1,0:T(1,128)S(1)} async-done(((f32[32,1,128]{2,1,0:T(1,128)}), f32[32,1,128]{2,1,0:T(1,128)S(1)}, u32[]{:S(2)}, u32[]{:S(2)}) %all-to-all-start.1) | async-done | bytes 16416 | tf_op jit(solution)/shard_map/all_to_all | solution.py:314
  34.9 0.8 %finish.1 = (bf16[8,1024]{1,0:T(8,128)(2,1)}, f32[8,1024]{1,0:T(8,128)}) custom-call(f32[8,1024]{1,0:T(8,128)S(1)} %get-tuple-element.5.own.base, f32[32,1,128]{2,1,0:T(1,128)S(1)} %all-to-all-done.1.gram_parts, bf16[8,1024]{1,0:T(8,128)(2,1)S(1)} %copy-done, bf16[8,1024]{1,0:T(8,128)(2,1)S(1)} %collective-permute-done.2.refs_0_), custom_call_target="tpu_custom_call" | custom-call | tf_op jit(solution)/shard_map/finish/pallas_call | solution.py:258
Async XLA Ops:
  0.6 21.0 %copy-start = (bf16[8,1024]{1,0:T(8,128)(2,1)S(1)}, bf16[8,1024]{1,0:T(8,128)(2,1)}, u32[]{:S(2)}) copy-start(bf16[8,1024]{1,0:T(8,128)(2,1)} %vec.3) | copy-start | bytes 49156
  16.1 2.2 %collective-permute-start = (bf16[8,8,1024]{2,1,0:T(8,128)(2,1)S(1)}, bf16[8,8,1024]{2,1,0:T(8,128)(2,1)S(1)}, u32[]{:S(2)}, u32[]{:S(2)}) collective-permute-start(bf16[8,8,1024]{2,1,0:T(8,128)(2,1)S(1)} %all_to_all.10.refs_0_), channel_id=1, source_target_pairs={{0,2},{2,0},{1,3},{3,1},{4,6},{6,4},{5,7},{7,5},{8,10},{10,8},{9,1... | collective-permute-start | bytes 393224 | tf_op jit(solution)/shard_map/ppermute | solution.py:275
  16.1 5.4 %collective-permute-start.1 = (bf16[8,1024]{1,0:T(8,128)(2,1)}, bf16[8,1024]{1,0:T(8,128)(2,1)S(1)}, u32[]{:S(2)}, u32[]{:S(2)}) collective-permute-start(bf16[8,1024]{1,0:T(8,128)(2,1)} %vec.3), channel_id=1, source_target_pairs={{0,1},{1,0},{2,3},{3,2},{4,5},{5,4},{6,7},{7,6},{8,9},{9,8},{10,11... | collective-permute-start | bytes 49160 | tf_op jit(solution)/shard_map/ppermute | solution.py:275
  22.5 12.3 %all-to-all-start.1 = ((f32[32,1,128]{2,1,0:T(1,128)}), f32[32,1,128]{2,1,0:T(1,128)S(1)}, u32[]{:S(2)}, u32[]{:S(2)}) async-start(f32[32,1,128]{2,1,0:T(1,128)} %gram_terms.1), calls=%async_computation.1 | async-start | bytes 32768 | tf_op jit(solution)/shard_map/all_to_all | solution.py:314
  27.7 3.8 %collective-permute-start.2 = (bf16[8,1024]{1,0:T(8,128)(2,1)S(1)}, bf16[8,1024]{1,0:T(8,128)(2,1)S(1)}, u32[]{:S(2)}, u32[]{:S(2)}) collective-permute-start(bf16[8,1024]{1,0:T(8,128)(2,1)S(1)} %bitcast.2), channel_id=1, source_target_pairs={{0,1},{1,0},{2,3},{3,2},{4,5},{5,4},{6,7},{7,6},{8,9},{9,8},{10,11... | collective-permute-start | bytes 49160 | tf_op jit(solution)/shard_map/ppermute | solution.py:308
where the time goes:
time: 35.9 us; the launch traced here: 35.6 us
  blocking collectives  14.4 us (40%)
  starting transfers between devices  8.56 us (24%)
  Pallas kernels  6.02 us (17%)
  waiting for transfers between devices  5.29 us (15%)
  between operations  1.34 us (4%)
    all_to_all x1, blocking collectives, per_device(): gath = lax.all_to_all(repeat(vectors, lax.axis_size('far')), 'far', 0, 0)  14.4 us
    all_to_all x1, starting transfers between devices, per_device(): gram_parts = lax.all_to_all(terms, ('far', 'core', 'col'), 0, 0)  5.2 us
    all_to_all x1, waiting for transfers between devices, per_device(): gram_parts = lax.all_to_all(terms, ('far', 'core', 'col'), 0, 0)  3.3 us
    pallas_call x1, Pallas kernels, tile_work(): pl.pallas_call(functools.partial(tile_kernel, n_core, n_col, side), out_s...  3.25 us
    ppermute x1, waiting for transfers between devices, per_device(): lax.ppermute(send[s - 1], 'col', [(c, (c + s) % n_col) for c in range(n_c...  1.99 us
    ppermute x1, starting transfers between devices, per_device(): lax.ppermute(send[s - 1], 'col', [(c, (c + s) % n_col) for c in range(n_c...  1.83 us
    ppermute x2, starting transfers between devices, from_all(): lax.ppermute(x, axis, [(i, (i + s) % size) for i in range(size)])  1.52 us
    pallas_call x1, Pallas kernels, repeat(): pl.pallas_call(copies_kernel, out_shape=jax.ShapeDtypeStruct((size,) + x....  1.1 us
  transfers between devices with their start and end apart: 4, of which 2 were waited for; matrix products, arithmetic and copies ran while one was open for 0% of the time, Pallas kernels for 9%

commit v1 on v0

--- a/solution.py
+++ b/solution.py
@@ -20,7 +20,7 @@
 ):
     gath, refs = refs[:n_core], refs[n_core:]
     (own_ref, send_ref, rest_ref, rows_s, cols_s, ener,
-     buf, table, picked, select, part, sems, small, *acc) = refs
+     table, picked, select, part, small, *acc) = refs
     n_far, kvec, own = gath[0].shape
     slots = tiles.shape[0]
     blk_own = own // side
@@ -37,18 +37,8 @@
     for copy in copies:
         copy.start()
 
-    def tile_copy(ch):
-        span = pl.ds(pl.multiple_of(ch * CHUNK, CHUNK), CHUNK)
-        return pltpu.make_async_copy(tiles.at[span], buf.at[span], sems.at[ch])
-
     count = count_s[0]
     used = (count + CHUNK - 1) // CHUNK
-
-    def start(ch, carry):
-        tile_copy(ch).start()
-        return carry
-
-    lax.fori_loop(0, used, start, 0)
 
     lane = lax.broadcasted_iota(jnp.int32, (kvec, LANES), 1)
     low = lane < side
@@ -109,11 +99,10 @@
             acc[t][r] += out[t * rows_of:(t + 1) * rows_of]
 
     def one_chunk(ch, carry):
-        tile_copy(ch).wait()
         waiting = None
         for q in range(CHUNK // (2 * SUB)):
             base = pl.multiple_of(ch * CHUNK + q * 2 * SUB, 2 * SUB)
-            x = buf[pl.ds(base, 2 * SUB), :].astype(jnp.float32)
+            x = tiles[pl.ds(base, 2 * SUB), :].astype(jnp.float32)
             for half in range(2):
                 out = product(base, half, x)
                 if waiting is not None:
@@ -157,6 +146,43 @@
         rest_ref[s - 1] = share
 
 
+def fetch_kernel(count_s, tiles, buf, sems):
+    used = (count_s[0] + CHUNK - 1) // CHUNK
+
+    def tile_copy(ch):
+        span = pl.ds(pl.multiple_of(ch * CHUNK, CHUNK), CHUNK)
+        return pltpu.make_async_copy(tiles.at[span], buf.at[span], sems.at[ch])
+
+    def start(ch, carry):
+        tile_copy(ch).start()
+        return carry
+
+    def wait(ch, carry):
+        tile_copy(ch).wait()
+        return carry
+
+    lax.fori_loop(0, used, start, 0)
+    lax.fori_loop(0, used, wait, 0)
+
+
+def fetch_tiles(count, tiles):
+    return pl.pallas_call(
+        fetch_kernel,
+        out_shape=jax.ShapeDtypeStruct(tiles.shape, tiles.dtype),
+        in_specs=[
+            pl.BlockSpec(memory_space=pltpu.SMEM),
+            pl.BlockSpec(memory_space=pltpu.HBM),
+        ],
+        out_specs=pl.BlockSpec(memory_space=pltpu.VMEM),
+        scratch_shapes=[pltpu.SemaphoreType.DMA((tiles.shape[0] // CHUNK,))],
+        compiler_params=pltpu.CompilerParams(vmem_limit_bytes=12 * 2**20),
+        cost_estimate=pl.CostEstimate(
+            flops=0, bytes_accessed=4 * math.prod(tiles.shape), transcendentals=0
+        ),
+        name="fetch_tiles",
+    )(count, pltpu.with_memory_space_constraint(tiles, pltpu.HBM))
+
+
 def tile_work(rows, cols, count, gath, n_col, ener, tiles):
     n_core = len(gath)
     n_far, kvec, own = gath[0].shape
@@ -175,26 +201,25 @@
             jax.ShapeDtypeStruct((n_col - 1, kvec, own), jnp.bfloat16),
             jax.ShapeDtypeStruct((n_col - 1, kvec, own), jnp.float32),
         ),
-        in_specs=[pl.BlockSpec(memory_space=pltpu.SMEM)] + [far_away] * 4 + [vmem] * n_core,
+        in_specs=[pl.BlockSpec(memory_space=pltpu.SMEM)] + [far_away] * 3 + [vmem] + [vmem] * n_core,
         out_specs=(vmem, vmem, vmem),
         scratch_shapes=[
             pltpu.SMEM((slots,), jnp.int32),
             pltpu.SMEM((slots,), jnp.int32),
             pltpu.VMEM((1, own), jnp.float32),
-            pltpu.VMEM((slots, area), jnp.bfloat16),
             pltpu.VMEM((n_far * n_core * blk_own + 1, per * kvec, LANES), jnp.bfloat16),
             pltpu.VMEM((n_seg // per * 2 * kvec, per * per * width), jnp.bfloat16),
             pltpu.VMEM((per * per * width, LANES), jnp.bfloat16),
             pltpu.VMEM((n_col, kvec, own), jnp.float32),
-            pltpu.SemaphoreType.DMA((slots // CHUNK,)),
             pltpu.SemaphoreType.DMA((3,)),
         ] + [pltpu.VMEM((n_seg, per * kvec, width), jnp.float32)] * SUB,
-        compiler_params=pltpu.CompilerParams(vmem_limit_bytes=48 * 2**20),
+        compiler_params=pltpu.CompilerParams(vmem_limit_bytes=32 * 2**20),
         cost_estimate=pl.CostEstimate(
             flops=2 * slots * area * kvec, bytes_accessed=2 * slots * area, transcendentals=0
         ),
         name="tile_work",
-    )(count, *[pltpu.with_memory_space_constraint(x, pltpu.HBM) for x in (rows, cols, ener, tiles)],
+    )(count, *[pltpu.with_memory_space_constraint(x, pltpu.HBM) for x in (rows, cols, ener)],
+      tiles,
       *gath)
 
 
@@ -299,10 +324,11 @@
 def per_device(vectors, energies, tiles, tile_rows, tile_cols, tile_count):
     kvec, own = vectors.shape
     n_col = lax.axis_size("col")
+    fetched = fetch_tiles(tile_count, tiles)
     gath = lax.all_to_all(repeat(vectors, lax.axis_size("far")), "far", 0, 0)
     gath = from_all(gath, "core")
     base, send, rest = tile_work(
-        tile_rows, tile_cols, tile_count, gath, n_col, energies[None, :], tiles
+        tile_rows, tile_cols, tile_count, gath, n_col, energies[None, :], fetched
     )
     got = [
         lax.ppermute(send[s - 1], "col", [(c, (c + s) % n_col) for c in range(n_col)])

time: 35.9 us -> 39 us (1.086)
  Pallas kernels: 6.02 us -> 9.46 us
  starting transfers between devices: 8.56 us -> 7.87 us
    pallas_call x0 -> x1, Pallas kernels: none -> 2.31 us  [fetch_tiles(): pl.pallas_call(fetch_kernel, out_shape=jax.ShapeDtypeStruct(tiles.shape,...]
    pallas_call x1, Pallas kernels: 3.25 us -> 4.4 us  [tile_work(): pl.pallas_call(functools.partial(tile_kernel, n_core, n_col, side), out_s...]
    all_to_all x1, starting transfers between devices: 5.2 us -> 4.51 us  [per_device(): gram_parts = lax.all_to_all(terms, ('far', 'core', 'col'), 0, 0)]
  transfers between devices with their start and end apart: 4 -> 4, of which waited for: 2 -> 2; matrix products, arithmetic and copies ran while one was open for 0% -> 0% of each run, Pallas kernels for 9% -> 17%
where the time goes in v1:
time: 39 us; the launch traced here: 38.4 us
  blocking collectives  14.4 us (37%)
  Pallas kernels  9.46 us (24%)
  starting transfers between devices  7.87 us (20%)
  waiting for transfers between devices  5.29 us (14%)
  between operations  1.35 us (3%)
    all_to_all x1, blocking collectives, per_device(): gath = lax.all_to_all(repeat(vectors, lax.axis_size('far')), 'far', 0, 0)  14.4 us
    all_to_all x1, starting transfers between devices, per_device(): gram_parts = lax.all_to_all(terms, ('far', 'core', 'col'), 0, 0)  4.51 us
    pallas_call x1, Pallas kernels, tile_work(): pl.pallas_call(functools.partial(tile_kernel, n_core, n_col, side), out_s...  4.4 us
    all_to_all x1, waiting for transfers between devices, per_device(): gram_parts = lax.all_to_all(terms, ('far', 'core', 'col'), 0, 0)  3.3 us
    pallas_call x1, Pallas kernels, fetch_tiles(): pl.pallas_call(fetch_kernel, out_shape=jax.ShapeDtypeStruct(tiles.shape,...  2.31 us
    ppermute x1, waiting for transfers between devices, per_device(): lax.ppermute(send[s - 1], 'col', [(c, (c + s) % n_col) for c in range(n_c...  1.99 us
    ppermute x1, starting transfers between devices, per_device(): lax.ppermute(send[s - 1], 'col', [(c, (c + s) % n_col) for c in range(n_c...  1.83 us
    ppermute x2, starting transfers between devices, from_all(): lax.ppermute(x, axis, [(i, (i + s) % size) for i in range(size)])  1.52 us
  transfers between devices with their start and end apart: 4, of which 2 were waited for; matrix products, arithmetic and copies ran while one was open for 0% of the time, Pallas kernels for 17%

profile of v1, /device:TPU:0, one launch (start us, length us, event | category | flops | bytes accessed | tf_op | source)
XLA Modules:
  0.0 38.4 jit_solution(1371468257987640773)
XLA Ops:
  0.6 1.1 %copies.1 = bf16[8,8,1024]{2,1,0:T(8,128)(2,1)S(1)} custom-call(bf16[8,1024]{1,0:T(8,128)(2,1)} %vec.3), custom_call_target="tpu_custom_call" | custom-call | tf_op jit(solution)/shard_map/copies/pallas_call | solution.py:313
  1.7 14.4 %all_to_all.10.refs_0_ = bf16[8,8,1024]{2,1,0:T(8,128)(2,1)S(1)} all-to-all(bf16[8,8,1024]{2,1,0:T(8,128)(2,1)S(1)} %copies.1), channel_id=1, replica_groups=mesh['far'=8,'core'=2,'col'=2] {'far'}, dimensions={0} | all-to-all | bytes 262144 | tf_op jit(solution)/shard_map/all_to_all | solution.py:328
  16.1 0.0 collective-permute-start
  16.1 1.5 %collective-permute-start.1 = (bf16[8,1024]{1,0:T(8,128)(2,1)}, bf16[8,1024]{1,0:T(8,128)(2,1)S(1)}, u32[]{:S(2)}, u32[]{:S(2)}) collective-permute-start(bf16[8,1024]{1,0:T(8,128)(2,1)} %vec.3), channel_id=1, source_target_pairs={{0,1},{1,0},{2,3},{3,2},{4,5},{5,4},{6,7},{7,6},{8,9},{9,8},{10,11... | collective-permute-start | bytes 49160 | tf_op jit(solution)/shard_map/ppermute | solution.py:300
  18.3 2.3 %fetch_tiles.1.tiles = bf16[1024,4096]{1,0:T(8,128)(2,1)S(1)} custom-call(s32[1]{0:T(128)S(6)} %copy.8.count_s, bf16[1024,4096]{1,0:T(8,128)(2,1)} %tiles.1), custom_call_target="tpu_custom_call" | custom-call | bytes 16777216 | tf_op jit(solution)/shard_map/fetch_tiles/pallas_call | solution.py:169
  20.6 0.0 copy-start
  20.6 0.0 collective-permute-done.refs_1_
  20.6 4.4 %tile_work.1 = (f32[8,1024]{1,0:T(8,128)S(1)}, bf16[1,8,1024]{2,1,0:T(8,128)(2,1)S(1)}, f32[1,8,1024]{2,1,0:T(8,128)S(1)}) custom-call(s32[1]{0:T(128)S(6)} %copy.8.count_s, s32[1024]{0:T(1024)} %rows_h.1, s32[1024]{0:T(1024)} %cols_h.1, f32[1,1024]{1,0:T(1,128)} %bitcast.3, bf16[1024,4096]{1,0:T(8,128)(2,1)S(1)} %fetch_tiles.1.tiles, ...), custom_call_target="tpu_custom_call" | custom-call | flops 67108864 | bytes 8388608 | tf_op jit(solution)/shard_map/tile_work/pallas_call | solution.py:197
  25.0 0.0 collective-permute-done.1.refs_0_
  25.0 0.0 copy-done
  25.0 0.9 %gram_terms.1 = f32[32,1,128]{2,1,0:T(1,128)} custom-call(f32[8,1024]{1,0:T(8,128)S(1)} %get-tuple-element.5.own.base, f32[1,8,1024]{2,1,0:T(8,128)S(1)} %get-tuple-element.6.rest, bf16[8,1024]{1,0:T(8,128)(2,1)S(1)} %copy-done, bf16[8,1024]{1,0:T(8,128)(2,1)S(1)} %collective-permute-done.1.refs_0_), custom_call_target="tpu_custom_call" | custom-call | tf_op jit(solution)/shard_map/gram_terms/pallas_call | solution.py:250
  26.0 4.5 %all-to-all-start.1 = ((f32[32,1,128]{2,1,0:T(1,128)}), f32[32,1,128]{2,1,0:T(1,128)S(1)}, u32[]{:S(2)}, u32[]{:S(2)}) async-start(f32[32,1,128]{2,1,0:T(1,128)} %gram_terms.1), calls=%async_computation.1 | async-start | bytes 32768 | tf_op jit(solution)/shard_map/all_to_all | solution.py:340
  30.5 1.8 %collective-permute-start.2 = (bf16[8,1024]{1,0:T(8,128)(2,1)S(1)}, bf16[8,1024]{1,0:T(8,128)(2,1)S(1)}, u32[]{:S(2)}, u32[]{:S(2)}) collective-permute-start(bf16[8,1024]{1,0:T(8,128)(2,1)S(1)} %bitcast.2), channel_id=1, source_target_pairs={{0,1},{1,0},{2,3},{3,2},{4,5},{5,4},{6,7},{7,6},{8,9},{9,8},{10,11... | collective-permute-start | bytes 49160 | tf_op jit(solution)/shard_map/ppermute | solution.py:334
  32.3 2.0 %collective-permute-done.2.refs_0_ = bf16[8,1024]{1,0:T(8,128)(2,1)S(1)} collective-permute-done((bf16[8,1024]{1,0:T(8,128)(2,1)S(1)}, bf16[8,1024]{1,0:T(8,128)(2,1)S(1)}, u32[]{:S(2)}, u32[]{:S(2)}) %collective-permute-start.2) | collective-permute-done | bytes 16416 | tf_op jit(solution)/shard_map/ppermute | solution.py:334
  34.3 3.3 %all-to-all-done.1.gram_parts = f32[32,1,128]{2,1,0:T(1,128)S(1)} async-done(((f32[32,1,128]{2,1,0:T(1,128)}), f32[32,1,128]{2,1,0:T(1,128)S(1)}, u32[]{:S(2)}, u32[]{:S(2)}) %all-to-all-start.1) | async-done | bytes 16416 | tf_op jit(solution)/shard_map/all_to_all | solution.py:340
  37.6 0.8 %finish.1 = (bf16[8,1024]{1,0:T(8,128)(2,1)}, f32[8,1024]{1,0:T(8,128)}) custom-call(f32[8,1024]{1,0:T(8,128)S(1)} %get-tuple-element.5.own.base, f32[32,1,128]{2,1,0:T(1,128)S(1)} %all-to-all-done.1.gram_parts, bf16[8,1024]{1,0:T(8,128)(2,1)S(1)} %copy-done, bf16[8,1024]{1,0:T(8,128)(2,1)S(1)} %collective-permute-done.2.refs_0_), custom_call_target="tpu_custom_call" | custom-call | tf_op jit(solution)/shard_map/finish/pallas_call | solution.py:283
Async XLA Ops:
  16.1 4.5 %collective-permute-start = (bf16[8,8,1024]{2,1,0:T(8,128)(2,1)S(1)}, bf16[8,8,1024]{2,1,0:T(8,128)(2,1)S(1)}, u32[]{:S(2)}, u32[]{:S(2)}) collective-permute-start(bf16[8,8,1024]{2,1,0:T(8,128)(2,1)S(1)} %all_to_all.10.refs_0_), channel_id=1, source_target_pairs={{0,2},{2,0},{1,3},{3,1},{4,6},{6,4},{5,7},{7,5},{8,10},{10,8},{9,1... | collective-permute-start | bytes 393224 | tf_op jit(solution)/shard_map/ppermute | solution.py:300
  16.1 8.9 %collective-permute-start.1 = (bf16[8,1024]{1,0:T(8,128)(2,1)}, bf16[8,1024]{1,0:T(8,128)(2,1)S(1)}, u32[]{:S(2)}, u32[]{:S(2)}) collective-permute-start(bf16[8,1024]{1,0:T(8,128)(2,1)} %vec.3), channel_id=1, source_target_pairs={{0,1},{1,0},{2,3},{3,2},{4,5},{5,4},{6,7},{7,6},{8,9},{9,8},{10,11... | collective-permute-start | bytes 49160 | tf_op jit(solution)/shard_map/ppermute | solution.py:300
  20.6 4.4 %copy-start = (bf16[8,1024]{1,0:T(8,128)(2,1)S(1)}, bf16[8,1024]{1,0:T(8,128)(2,1)}, u32[]{:S(2)}) copy-start(bf16[8,1024]{1,0:T(8,128)(2,1)} %vec.3) | copy-start | bytes 49156
  26.0 11.6 %all-to-all-start.1 = ((f32[32,1,128]{2,1,0:T(1,128)}), f32[32,1,128]{2,1,0:T(1,128)S(1)}, u32[]{:S(2)}, u32[]{:S(2)}) async-start(f32[32,1,128]{2,1,0:T(1,128)} %gram_terms.1), calls=%async_computation.1 | async-start | bytes 32768 | tf_op jit(solution)/shard_map/all_to_all | solution.py:340
  30.5 3.8 %collective-permute-start.2 = (bf16[8,1024]{1,0:T(8,128)(2,1)S(1)}, bf16[8,1024]{1,0:T(8,128)(2,1)S(1)}, u32[]{:S(2)}, u32[]{:S(2)}) collective-permute-start(bf16[8,1024]{1,0:T(8,128)(2,1)S(1)} %bitcast.2), channel_id=1, source_target_pairs={{0,1},{1,0},{2,3},{3,2},{4,5},{5,4},{6,7},{7,6},{8,9},{9,8},{10,11... | collective-permute-start | bytes 49160 | tf_op jit(solution)/shard_map/ppermute | solution.py:334
